TPU v7x, 128 devices: a whole 4x4x4 slice. The times are simulated.
128 devices in a mesh: src: 8 (over y, core), rcv: 16 (over x, z).
Axes of the slice: x: 4, y: 4, z: 4, core: 2. Of those that a mesh axis runs over, the one named last changes fastest.
Arguments:
- traces: bfloat16 [65536, 2048], P('rcv', 'src'), may hold values from -32 to 32
- tile_list: int32 [252, 2], replicated, may hold values from 0 to 31, as said below
- tile_owner: int32 [512], replicated, may hold values from 0 to 252, as said below
Outputs:
- stacked: bfloat16 [512, 64, 64, 512], P(('src', 'rcv'))
Inputs may be any that keep to these rules, and one draw needn't show every extreme that they name: `tile_list`: every tile (s, r) with s <= r <= s + 8 and r < 32 appears in exactly one row. `tile_owner`: slots k with k // 4 = d belong to device d of src+rcv in mesh order; the value 252 marks an empty slot; every tile is held in exactly one slot, and some device holds 4 tiles.
All inputs are finite; a program needn't handle non-finite values.
Results may differ from a plain program's by a relative error of at most 0.0065.
Values may be sent and summed in bfloat16 or wider, within the bound.
A program may use at most 384 MiB of HBM per device.

v0:
```python
import math

import jax
import jax.numpy as jnp
from jax import lax
from jax.sharding import PartitionSpec as P

SAMPLES = 2048
BINS = 256
LOW_BIN = 16
BLOCK = 64


def spectral_basis():
    sample_index = jnp.arange(SAMPLES, dtype=jnp.int32)
    bin_index = LOW_BIN + jnp.arange(BINS, dtype=jnp.int32)
    turns = sample_index[:, None] * bin_index[None, :] % SAMPLES
    angle = 2.0 * math.pi / SAMPLES * turns.astype(jnp.float32)
    return jnp.concatenate([jnp.cos(angle), -jnp.sin(angle)], axis=1).astype(jnp.bfloat16)


def transform(frames, basis):
    window_count = frames.shape[0] // SAMPLES
    shaped = frames.reshape(window_count, SAMPLES, frames.shape[1])
    spectrum = jnp.einsum("wlc,lk->wck", shaped, basis, preferred_element_type=jnp.float32)
    mean_power = jnp.mean(spectrum * spectrum, axis=-1, keepdims=True)
    return (spectrum * lax.rsqrt(mean_power + 1e-06)).astype(jnp.bfloat16)


def product(left, right):
    return jnp.einsum("wkif,wkjf->kijf", left, right, preferred_element_type=jnp.float32)


def cross_pairs(source, target):
    window_total = source.shape[0]
    source_re, source_im = (source[..., :BINS], source[..., BINS:])
    target_re, target_im = (target[..., :BINS], target[..., BINS:])
    real_part = (product(source_re, target_re) + product(source_im, target_im)) / window_total
    imag_part = (product(source_im, target_re) - product(source_re, target_im)) / window_total
    return jnp.concatenate([real_part, imag_part], axis=-1).astype(jnp.bfloat16)


def cross_slots(received):
    return cross_pairs(received[:, 0, :, 0], received[:, 0, :, 1])


def pairs_of(owners, tile_list):
    tile_count = tile_list.shape[0]
    clipped = jnp.minimum(owners, tile_count - 1)
    picked = (clipped[:, None] == jnp.arange(tile_count, dtype=jnp.int32)[None, :]).astype(
        jnp.int32
    )
    return jnp.sum(picked[:, :, None] * tile_list[None, :, :], axis=1)


def per_device(traces, tile_list, tile_owner):
    basis = spectral_basis()
    spectra = lax.all_gather(transform(traces, basis), "src", axis=1, tiled=True)
    src_count = lax.axis_size("src")
    rcv_count = lax.axis_size("rcv")
    device_count = src_count * rcv_count
    slots_dev = tile_owner.shape[0] // device_count
    tile_count = tile_list.shape[0]
    local_windows = spectra.shape[0]
    blocked = spectra.reshape(local_windows, spectra.shape[1] // BLOCK, BLOCK, 2 * BINS)
    row_start = lax.axis_index("src") * (rcv_count * slots_dev)
    row_owner = lax.dynamic_slice_in_dim(tile_owner, row_start, rcv_count * slots_dev)
    block_pairs = pairs_of(row_owner, tile_list)
    outgoing = jnp.take(blocked, block_pairs.reshape(-1), axis=1)
    outgoing = outgoing.reshape(local_windows, rcv_count, slots_dev, 2, BLOCK, 2 * BINS)
    crossed = cross_slots(lax.all_to_all(outgoing, "rcv", split_axis=1, concat_axis=0, tiled=True))
    device_slot = (lax.axis_index("src") * rcv_count + lax.axis_index("rcv")) * slots_dev
    own_slots = lax.dynamic_slice_in_dim(tile_owner, device_slot, slots_dev)
    filled = (own_slots < tile_count).astype(jnp.bfloat16)
    return crossed * filled[:, None, None, None]


def solution(mesh):
    in_specs = (P("rcv", "src"), P(), P())
    out_specs = P(("src", "rcv"), None, None, None)
    return jax.shard_map(
        per_device, mesh=mesh, in_specs=in_specs, out_specs=out_specs, check_vma=False
    )
```

profile of v0, /device:TPU:1, one launch (start us, length us, event | category | flops | bytes accessed | tf_op | source)
XLA Modules:
  0.0 709.8 jit_solution(2125195099265088094)
XLA Ops:
  6.5 0.0 copy-start
  6.5 9.0 %cosine_convert_fusion = (bf16[2048,256]{0,1:T(8,128)(2,1)S(1)}, bf16[2048,256]{0,1:T(8,128)(2,1)S(1)}) fusion(s32[256]{0:T(256)S(1)} %iota_add_fusion), kind=kLoop, calls=%fused_computation.28 | loop fusion | flops 8912896 | bytes 2098176 | tf_op jit(solution)/shard_map/convert.4
  15.5 0.0 copy-done
  15.5 1.3 multiply_reduce_fusion
  16.8 0.9 fusion.19
  17.7 0.0 all-gather.2.cloned.1.call-update
  17.8 0.8 dynamic-slice_minimum_fusion
  18.5 0.1 fusion.20
  18.6 0.1 multiply_reduce_fusion.1
  18.7 0.1 copy.30
  18.8 0.1 reshape.85
  18.9 0.1 reshape.88
  19.1 0.2 copy.28
  19.3 38.3 %all-gather.2.cloned.1.call-done = bf16[2,2048,512]{1,2,0:T(8,128)(2,1)} async-done(((bf16[2,256,512]{1,2,0:T(8,128)(2,1)}), bf16[2,2048,512]{1,2,0:T(8,128)(2,1)}) %all-gather.2.cloned.1.call-update) | async-done | bytes 4194320 | tf_op jit(solution)/shard_map/all_gather | solution.py:58
  57.6 6.3 copy.29
  63.9 10.5 %gather_fusion = bf16[128,2,64,512]{3,2,1,0:T(8,128)(2,1)} fusion(bf16[2,32,64,512]{3,2,1,0:T(8,128)(2,1)} %bitcast.34, s32[1024]{0:T(1024)S(1)} %pad_clamp_fusion), kind=kCustom, calls=%fused_computation | custom fusion | bytes 33554944 | tf_op jit(solution)/shard_map/jit(_take)/gather | solution.py:69
  74.4 14.1 %copy_select_fusion = bf16[2,16,4,2,64,512]{5,4,3,2,0,1:T(8,128)(2,1)} fusion(bf16[2,16,4,2,64,512]{5,4,0,3,2,1:T(8,128)(2,1)} %bitcast.40, pred[16,4,2]{2,1,0:T(4,128)(4,1)S(1)} %copy.28), kind=kLoop, calls=%fused_computation.4 | loop fusion | flops 8388608 | bytes 33554560 | tf_op jit(solution)/shard_map/jit(_take)/select_n | solution.py:69
  88.5 6.7 all-to-all-start
  95.3 1.3 compare_convert_fusion
  96.6 297.0 %all-to-all-done = bf16[2,16,4,2,64,512]{5,4,3,2,0,1:T(8,128)(2,1)} async-done(((bf16[2,16,4,2,64,512]{5,4,3,2,0,1:T(8,128)(2,1)}), bf16[2,16,4,2,64,512]{5,4,3,2,0,1:T(8,128)(2,1)}, u32[]{:S(2)}, u32[]{:S(2)}) %all-to-all-start) | async-done | bytes 16777248 | tf_op jit(solution)/shard_map/all_to_all | solution.py:71
  393.5 79.4 %copy.32 = bf16[16,2,1,4,2,64,512]{5,1,0,6,3,4,2:T(2,128)(2,1)} copy(bf16[16,2,1,4,2,64,512]{6,5,4,3,1,0,2:T(8,128)(2,1)} %bitcast.8) | data formatting | bytes 33554432 | tf_op jit(solution)/shard_map/all_to_all | solution.py:71
  472.9 8.9 %slice_bitcast_fusion = bf16[32,4,64,512]{2,0,3,1:T(8,128)(2,1)S(1)} fusion(bf16[32,1,4,2,64,512]{4,0,5,2,3,1:T(8,128)(2,1)} %bitcast.35), kind=kLoop, calls=%fused_computation.1 | loop fusion | bytes 16777216 | tf_op jit(solution)/shard_map/squeeze | solution.py:44
  481.8 14.9 %fusion.3 = f32[4,256,64,64]{3,2,1,0:T(8,128)} fusion(bf16[32,1,4,2,64,512]{4,0,5,2,3,1:T(8,128)(2,1)} %bitcast.36, bf16[32,4,64,512]{2,0,3,1:T(8,128)(2,1)S(1)} %slice_bitcast_fusion), kind=kOutput, calls=%fused_computation.10 | convolution fusion | flops 268435456 | bytes 41943040 | tf_op jit(solution)/shard_map/wkif,wkjf->kijf/dot_general | solution.py:31
  496.7 14.8 %fusion.2 = f32[4,256,64,64]{3,2,1,0:T(8,128)} fusion(bf16[32,1,4,2,64,512]{4,0,5,2,3,1:T(8,128)(2,1)} %bitcast.37, bf16[32,4,64,512]{2,0,3,1:T(8,128)(2,1)S(1)} %slice_bitcast_fusion), kind=kOutput, calls=%fused_computation.9 | convolution fusion | flops 268435456 | bytes 41943040 | tf_op jit(solution)/shard_map/wkif,wkjf->kijf/dot_general | solution.py:31
  511.5 14.8 %fusion = f32[4,256,64,64]{3,2,1,0:T(8,128)} fusion(bf16[32,1,4,2,64,512]{4,0,5,2,3,1:T(8,128)(2,1)} %bitcast.38, bf16[32,4,64,512]{2,0,3,1:T(8,128)(2,1)S(1)} %slice_bitcast_fusion), kind=kOutput, calls=%fused_computation.7 | convolution fusion | flops 268435456 | bytes 41943040 | tf_op jit(solution)/shard_map/wkif,wkjf->kijf/dot_general | solution.py:31
  526.4 14.8 %fusion.1 = f32[4,256,64,64]{3,2,1,0:T(8,128)} fusion(bf16[32,1,4,2,64,512]{4,0,5,2,3,1:T(8,128)(2,1)} %bitcast.39, bf16[32,4,64,512]{2,0,3,1:T(8,128)(2,1)S(1)} %slice_bitcast_fusion), kind=kOutput, calls=%fused_computation.8 | convolution fusion | flops 268435456 | bytes 41943040 | tf_op jit(solution)/shard_map/wkif,wkjf->kijf/dot_general | solution.py:31
  541.2 29.2 %copy.35 = f32[4,256,64,64]{1,2,3,0:T(8,128)} copy(f32[4,256,64,64]{3,2,1,0:T(8,128)} %fusion.3) | data formatting | bytes 33554432 | tf_op jit(solution)/shard_map/wkif,wkjf->kijf/dot_general | solution.py:31
  570.4 29.2 %copy.36 = f32[4,256,64,64]{1,2,3,0:T(8,128)} copy(f32[4,256,64,64]{3,2,1,0:T(8,128)} %fusion.2) | data formatting | bytes 33554432 | tf_op jit(solution)/shard_map/wkif,wkjf->kijf/dot_general | solution.py:31
  599.6 29.1 %copy.34 = f32[4,256,64,64]{1,2,3,0:T(8,128)} copy(f32[4,256,64,64]{3,2,1,0:T(8,128)} %fusion) | data formatting | bytes 33554432 | tf_op jit(solution)/shard_map/wkif,wkjf->kijf/dot_general | solution.py:31
  628.8 29.1 %copy.33 = f32[4,256,64,64]{1,2,3,0:T(8,128)} copy(f32[4,256,64,64]{3,2,1,0:T(8,128)} %fusion.1) | data formatting | bytes 33554432 | tf_op jit(solution)/shard_map/wkif,wkjf->kijf/dot_general | solution.py:31
  657.9 29.2 %fusion.4 = (bf16[4,64,64,256]{3,2,1,0:T(8,128)(2,1)}, bf16[4,64,64,256]{3,2,1,0:T(8,128)(2,1)}) fusion(f32[4,256,64,64]{1,2,3,0:T(8,128)} %copy.33, f32[4,256,64,64]{1,2,3,0:T(8,128)} %copy.34, f32[4,256,64,64]{1,2,3,0:T(8,128)} %copy.35, f32[4,256,64,64]{1,2,3,0:T(8,128)} %copy.36), kind=kLoop, calls=%fused_computation.11 | loop fusion | flops 25165824 | bytes 83886080 | tf_op jit(solution)/shard_map/div | solution.py:38
  687.0 15.9 %maximum_multiply_fusion = bf16[4,64,64,512]{3,2,1,0:T(8,128)(2,1)} fusion(bf16[4,64,64,256]{3,2,1,0:T(8,128)(2,1)} %get-tuple-element.10, bf16[4,64,64,256]{3,2,1,0:T(8,128)(2,1)} %get-tuple-element.9, bf16[4]{0:T(256)(128)(2,1)S(1)} %copy-done.3), kind=kLoop, calls=%fused_computation.3 | loop fusion | flops 50331648 | bytes 33554440 | tf_op jit(solution)/shard_map/mul | solution.py:75
  (12 shorter events, 0.0 us)
Async XLA Ops:
  6.5 9.0 %copy-start = (bf16[4096,256]{1,0:T(8,128)(2,1)S(1)}, bf16[4096,256]{1,0:T(8,128)(2,1)}, u32[]{:S(2)}) copy-start(bf16[4096,256]{1,0:T(8,128)(2,1)} %param.3) | copy-start | bytes 6291460
  6.5 12.1 %copy-start.2 = (s32[252,2]{0,1:T(2,128)S(1)}, s32[252,2]{0,1:T(2,128)}, u32[]{:S(2)}) copy-start(s32[252,2]{0,1:T(2,128)} %param.4) | copy-start | bytes 6052
  6.5 51.1 %all-gather.2.cloned.1.call-start = ((), (), s32[]{:S(2)}) async-start(), calls=%async_computation.1 | async-start | bytes 4718592 | tf_op jit(solution)/shard_map/all_gather | solution.py:58
  88.5 305.0 %all-to-all-start = ((bf16[2,16,4,2,64,512]{5,4,3,2,0,1:T(8,128)(2,1)}), bf16[2,16,4,2,64,512]{5,4,3,2,0,1:T(8,128)(2,1)}, u32[]{:S(2)}, u32[]{:S(2)}) async-start(bf16[2,16,4,2,64,512]{5,4,3,2,0,1:T(8,128)(2,1)} %copy_select_fusion), calls=%async_computation | async-start | bytes 33554432 | tf_op jit(solution)/shard_map/all_to_all | solution.py:71
  657.9 29.2 %copy-start.3 = (bf16[4]{0:T(256)(128)(2,1)S(1)}, bf16[4]{0:T(256)(128)(2,1)}, u32[]{:S(2)}) copy-start(bf16[4]{0:T(256)(128)(2,1)} %compare_convert_fusion) | copy-start | bytes 28
  687.0 15.9 %copy-start.1 = (bf16[4096,256]{1,0:T(8,128)(2,1)S(1)}, bf16[4096,256]{1,0:T(8,128)(2,1)}, u32[]{:S(2)}) copy-start(bf16[4096,256]{1,0:T(8,128)(2,1)} %param.3) | copy-start | bytes 6291460
Sparse Core Ops, SparseCore 0:
  17.9 39.6 all-gather.1
where the time goes:
time: 715 us; the launch traced here: 710 us
  waiting for transfers between devices  335 us (47%)
  local copies, waits for them, and re-layouts  222 us (31%)
  other arithmetic  71.3 us (10%)
  matrix products  60.7 us (8%)
  between operations  13.5 us (2%)
    all_to_all x1, waiting for transfers between devices, per_device(): lax.all_to_all(outgoing, 'rcv', split_axis=1, concat_axis=0, tiled=True)  297 us
    dot_general x4, local copies, waits for them, and re-layouts, product(): jnp.einsum('wkif,wkjf->kijf', left, right, preferred_element_type=jnp.flo...  117 us
    all_to_all x1, local copies, waits for them, and re-layouts, per_device(): lax.all_to_all(outgoing, 'rcv', split_axis=1, concat_axis=0, tiled=True)  79.4 us
    dot_general x4, matrix products, product(): jnp.einsum('wkif,wkjf->kijf', left, right, preferred_element_type=jnp.flo...  59.4 us
    all_gather x1, waiting for transfers between devices, per_device(): lax.all_gather(transform(traces, basis), 'src', axis=1, tiled=True)  38.3 us
    div x1, other arithmetic, cross_pairs(): (product(source_re, target_re) + product(source_im, target_im)) / window_...  29.2 us
    mul x1, other arithmetic, per_device(): return crossed * filled[:, None, None, None]  15.9 us
  transfers between devices with their start and end apart: 2, of which 2 were waited for; matrix products, arithmetic and copies ran while one was open for 0% of the time, Pallas kernels for 0%

commit v1 on v0

v1 whole, which is shorter than its diff:
```python
import functools
import math

import jax
import jax.numpy as jnp
import numpy as np
from jax import lax
from jax.experimental import pallas as pl
from jax.experimental.pallas import tpu as pltpu
from jax.sharding import PartitionSpec as P

SAMPLES = 2048
BINS = 256
LOW_BIN = 16
BLOCK = 64
TILES = 252
GROUPS = BINS // 8
CHUNKS = 4
FG = GROUPS // 4 // CHUNKS
ENTRIES = 16
MESH = pl.DeviceIdType.MESH
BF16 = jnp.bfloat16
F32 = jnp.float32


def twiddles():
    k = LOW_BIN + np.arange(BINS)[:, None]
    coarse = 2.0 * math.pi * ((k * 128 * np.arange(SAMPLES // 128)[None, :]) % SAMPLES) / SAMPLES
    fine = 2.0 * math.pi * ((k * np.arange(128)[None, :]) % SAMPLES) / SAMPLES
    pad = ((0, 0), (0, 128 - SAMPLES // 128))
    tables = [np.pad(np.cos(coarse), pad), np.pad(np.sin(coarse), pad), np.cos(fine), np.sin(fine)]
    return np.stack(tables).astype(np.float32)


def transform_kernel(traces_ref, table_ref, out_ref, basis_ref):
    cos_fine, sin_fine = table_ref[2], table_ref[3]
    for step in range(SAMPLES // 128):
        cos_coarse = table_ref[0, :, step : step + 1]
        sin_coarse = table_ref[1, :, step : step + 1]
        lanes = pl.ds(step * 128, 128)
        basis_ref[:BINS, lanes] = (cos_coarse * cos_fine - sin_coarse * sin_fine).astype(BF16)
        basis_ref[BINS:, lanes] = (-(sin_coarse * cos_fine + cos_coarse * sin_fine)).astype(BF16)
    whitened = []
    for window in range(2):
        spectrum = jnp.dot(
            basis_ref[...], traces_ref[window * SAMPLES : (window + 1) * SAMPLES, :],
            preferred_element_type=F32,
        )
        power = jnp.sum(spectrum * spectrum, axis=0, keepdims=True) * (1.0 / (2 * BINS))
        whitened.append(spectrum * lax.rsqrt(power + 1e-06))
    for block in range(4):
        lanes = slice(block * BLOCK, (block + 1) * BLOCK)
        rows = [
            jnp.concatenate([w[:BINS, lanes], w[BINS:, lanes]], axis=1).reshape(GROUPS, 8, 128)
            for w in whitened
        ]
        out_ref[block] = jnp.concatenate(rows, axis=1).astype(BF16)


def transform(traces):
    return pl.pallas_call(
        transform_kernel,
        name="transform",
        out_shape=jax.ShapeDtypeStruct((4, GROUPS, 16, 128), BF16),
        in_specs=[pl.BlockSpec(memory_space=pltpu.VMEM)] * 2,
        out_specs=pl.BlockSpec(memory_space=pltpu.VMEM),
        scratch_shapes=[pltpu.VMEM((2 * BINS, SAMPLES), BF16)],
        compiler_params=pltpu.CompilerParams(vmem_limit_bytes=40 * 2**20),
    )(traces, twiddles())


def gather_kernel(owner_ref, tiles_ref, spec_ref, out_ref, *scratch):
    count = 2 * CHUNKS
    held = scratch[:count]
    stage = scratch[count : 2 * count]
    final = scratch[2 * count : 3 * count]
    swap_s, swap_r, one_s, one_r, two_s, two_r, three_s, three_r, sib_s, sib_r, out_s = scratch[3 * count :]
    src, rcv = lax.axis_index("src"), lax.axis_index("rcv")
    y, core, x, z = src // 2, src % 2, rcv // 4, rcv % 4

    def device(axis, step):
        if axis == "core":
            return (y * 2 + (1 - core), rcv)
        if axis == "x":
            return (src, (x + step) % 4 * 4 + z)
        if axis == "y":
            return ((y + step) % 4 * 2 + core, rcv)
        return (src, x * 4 + (z + step) % 4)

    partners = [device("core", 0)] + [device(a, s) for a in "xyz" for s in (1, 2, 3)]
    barrier = pltpu.get_barrier_semaphore()
    for partner in partners:
        pl.semaphore_signal(barrier, inc=1, device_id=partner, device_id_type=MESH)

    for c in range(CHUNKS):
        for q in range(2):
            n = 2 * c + q
            mine = (x, z)[q]
            start = core * (GROUPS // 2) + q * (GROUPS // 4) + c * FG
            for block in range(4):
                held[n][y, mine, core * 4 + block] = spec_ref[block, pl.ds(start, FG)]
    pl.semaphore_wait(barrier, len(partners))

    sent = []

    def send(source, target, send_sem, recv_sem, to):
        copy = pltpu.make_async_remote_copy(
            src_ref=source, dst_ref=target, send_sem=send_sem, recv_sem=recv_sem,
            device_id=to, device_id_type=MESH,
        )
        copy.start()
        sent.append(copy)
        return copy

    order = [(c, q) for c in range(CHUNKS) for q in range(2)]
    swaps, ones, twos, threes, sibs, outs = {}, {}, {}, {}, {}, {}
    for c, q in order:
        n = 2 * c + q
        mine = (x, z)[q]
        start = (1 - core) * (GROUPS // 2) + q * (GROUPS // 4) + c * FG
        swaps[n] = send(
            spec_ref.at[:, pl.ds(start, FG)], held[n].at[y, mine, pl.ds(core * 4, 4)],
            swap_s.at[n], swap_r.at[n], device("core", 0),
        )
    for c, q in order:
        n = 2 * c + q
        mine = (x, z)[q]
        swaps[n].wait_recv()
        part = held[n].at[y, mine]
        ones[n] = [
            send(part, part, one_s.at[n, s - 1], one_r.at[n, s - 1], device("xz"[q], s))
            for s in (1, 3, 2)
        ]
    for c, q in order:
        n = 2 * c + q
        for copy in ones[n]:
            copy.wait_recv()
        part = held[n].at[y]
        twos[n] = [
            send(part, part, two_s.at[n, s - 1], two_r.at[n, s - 1], device("y", s))
            for s in (1, 3, 2)
        ]

    def finish(n):
        c, q = n // 2, n % 2
        for copy in threes[n]:
            copy.wait_recv()
        local = pltpu.make_async_copy(
            final[n].at[:, pl.ds(core * 8, 8)], out_ref.at[core, q, c], out_s.at[n]
        )
        local.start()
        outs[n] = local
        sibs[n] = send(
            final[n].at[:, pl.ds((1 - core) * 8, 8)], out_ref.at[core, q, c],
            sib_s.at[n], sib_r.at[n], device("core", 0),
        )

    for position, (c, q) in enumerate(order):
        n = 2 * c + q
        for copy in twos[n]:
            copy.wait_recv()
        last = (z, x)[q]

        def pick(e, step):
            there = (last + step) % 4
            to_rcv = (x * 4 + there, there * 4 + z)[q]
            slot = ((y * 2 + e // 8) * 16 + to_rcv) * 4 + e % 8 // 2
            tile = jnp.minimum(owner_ref[slot], TILES - 1)
            block = tiles_ref[2 * tile + e % 2]
            return held[n][block // 8, :, block % 8]

        for step in range(4):

            @pl.loop(0, ENTRIES)
            def _(e, step=step):
                if step:
                    stage[n][step - 1, e] = pick(e, step)
                else:
                    final[n][last, e] = pick(e, step)

        threes[n] = [
            send(
                stage[n].at[s - 1], final[n].at[last],
                three_s.at[n, s - 1], three_r.at[n, s - 1], device("zx"[q], s),
            )
            for s in (1, 3, 2)
        ]
        if position:
            finish(2 * order[position - 1][0] + order[position - 1][1])
    finish(2 * order[-1][0] + order[-1][1])
    for n in range(count):
        sibs[n].wait_recv()
        outs[n].wait()
    for copy in sent:
        copy.wait_send()


def gather(owner, tiles, spec):
    count = 2 * CHUNKS
    tail = (FG, 16, 128)
    dma = pltpu.SemaphoreType.DMA
    return pl.pallas_call(
        gather_kernel,
        name="gather",
        out_shape=jax.ShapeDtypeStruct((2, 2, CHUNKS, 4, 8, 4) + tail, BF16),
        in_specs=[
            pl.BlockSpec(memory_space=pltpu.SMEM),
            pl.BlockSpec(memory_space=pltpu.SMEM),
            pl.BlockSpec(memory_space=pltpu.VMEM),
        ],
        out_specs=pl.BlockSpec(memory_space=pl.ANY),
        scratch_shapes=[pltpu.VMEM((4, 4, 8) + tail, BF16)] * count
        + [pltpu.VMEM((3, ENTRIES, 4) + tail, BF16)] * count
        + [pltpu.VMEM((4, ENTRIES, 4) + tail, BF16)] * count
        + [dma((count,))] * 2
        + [dma((count, 3))] * 6
        + [dma((count,))] * 3,
        compiler_params=pltpu.CompilerParams(
            collective_id=0, has_side_effects=True, vmem_limit_bytes=56 * 2**20
        ),
    )(owner, tiles, spec)


def correlate_kernel(owner_ref, source_ref, target_ref, out_ref, cross_ref):
    slot, half = pl.program_id(0), pl.program_id(1)
    filled = owner_ref[slot] < TILES
    lane = lax.broadcasted_iota(jnp.int32, (BLOCK, 512), 1) % 8
    positive = lax.broadcasted_iota(jnp.int32, (256, 128), 1) < BLOCK
    sign = jnp.where(positive, 1.0, -1.0).astype(BF16)

    @pl.when(filled)
    def _():
        @pl.loop(0, 2 * CHUNKS, unroll=8 // FG)
        def _(step):
            q, c = step // CHUNKS, step % CHUNKS
            for group in range(FG):
                source = source_ref[0, q, c, :, 0, :, group].reshape(256, 128).T
                target = target_ref[0, q, c, :, 0, :, group].reshape(256, 128)
                left = jnp.concatenate([source[:BLOCK], source[BLOCK:]], axis=1)
                left = jnp.concatenate([jnp.where(lane == f, left, BF16(0)) for f in range(8)], axis=0)
                turned = jnp.concatenate([target[:, BLOCK:], target[:, :BLOCK]], axis=1)
                right = jnp.concatenate([target * sign, turned], axis=0)
                cross = jnp.dot(left, right, preferred_element_type=F32) * (1.0 / 32)
                first = pl.multiple_of(q * 64 + (c * FG + group) * 8, 8)
                cross_ref[:, pl.ds(first, 8), :] = jnp.swapaxes(cross.reshape(8, BLOCK, 128), 0, 1)

        @pl.loop(0, BLOCK, unroll=16)
        def _(i):
            turned = cross_ref[i].astype(BF16).T
            out_ref[0, i, :, pl.ds(pl.multiple_of(half * 128, 128), 128)] = turned[:BLOCK]
            out_ref[0, i, :, pl.ds(pl.multiple_of(BINS + half * 128, 128), 128)] = turned[BLOCK:]

    @pl.when(jnp.logical_not(filled))
    def _():
        out_ref[...] = jnp.zeros_like(out_ref)


def correlate(owner, received):
    block = (1, 2, CHUNKS, 4, 1, 4, FG, 16, 128)

    def side(role):
        return pl.BlockSpec(block, lambda s, k, own: (k, 0, 0, 0, 2 * s + role, 0, 0, 0, 0))

    return pl.pallas_call(
        correlate_kernel,
        name="correlate",
        out_shape=jax.ShapeDtypeStruct((4, BLOCK, BLOCK, 2 * BINS), BF16),
        grid_spec=pltpu.PrefetchScalarGridSpec(
            num_scalar_prefetch=1,
            grid=(4, 2),
            in_specs=[side(0), side(1)],
            out_specs=pl.BlockSpec((1, BLOCK, BLOCK, 2 * BINS), lambda s, k, own: (s, 0, 0, 0)),
            scratch_shapes=[pltpu.VMEM((BLOCK, 128, 128), F32)],
        ),
        compiler_params=pltpu.CompilerParams(vmem_limit_bytes=40 * 2**20),
    )(owner, received, received)


def per_device(traces, tile_list, tile_owner):
    spec = transform(traces)
    received = gather(tile_owner, tile_list.reshape(-1), spec)
    first = (lax.axis_index("src") * lax.axis_size("rcv") + lax.axis_index("rcv")) * 4
    return correlate(lax.dynamic_slice_in_dim(tile_owner, first, 4), received)


def solution(mesh):
    in_specs = (P("rcv", "src"), P(), P())
    out_specs = P(("src", "rcv"), None, None, None)
    return jax.shard_map(
        per_device, mesh=mesh, in_specs=in_specs, out_specs=out_specs, check_vma=False
    )
```

time: 715 us -> 188 us (0.26)
  the two profiles are of different devices: /device:TPU:1 before, /device:TPU:37 now
where the time goes in v1:
time: 188 us
  Pallas kernels  182 us (97%)
  local copies, waits for them, and re-layouts  5.69 us (3%)
    pallas_call x1, Pallas kernels, gather(): pl.pallas_call(gather_kernel, name='gather', out_shape=jax.ShapeDtypeStru...  146 us
    pallas_call x1, Pallas kernels, correlate(): pl.pallas_call(correlate_kernel, name='correlate', out_shape=jax.ShapeDty...  34.3 us
    unnamed x7, local copies, waits for them, and re-layouts  4.23 us

profile of v1, /device:TPU:37, one launch (start us, length us, event | category | flops | bytes accessed | tf_op | source)
XLA Modules:
  0.0 187.6 jit_solution(2404282163804846989)
XLA Ops:
  0.0 0.8 dynamic_slice.3.owner_ref
  0.8 0.8 copy.5
  1.6 0.7 reshape.3.tiles_ref
  2.3 0.0 copy-start
  2.3 1.6 copy-done
  3.9 0.0 copy-start.2
  3.9 1.0 copy-done.2
  4.9 2.0 %transform.1.spec_ref = bf16[4,32,16,128]{3,2,1,0:T(8,128)(2,1)S(1)} custom-call(bf16[4096,256]{1,0:T(8,128)(2,1)S(1)} %copy-done, f32[4,256,128]{2,1,0:T(8,128)S(1)} %copy-done.2), custom_call_target="tpu_custom_call" | custom-call | tf_op jit(solution)/shard_map/transform/pallas_call | solution.py:61
  6.9 0.0 copy-start.1
  6.9 0.8 copy-done.1
  7.7 145.6 %gather.1.source_ref.target_ref = bf16[2,2,4,4,8,4,2,16,128]{8,7,6,5,4,3,2,1,0:T(8,128)(2,1)} custom-call(s32[512]{0:T(512)} %owner_ref.1, s32[504]{0:T(512)} %reshape.3.tiles_ref, bf16[4,32,16,128]{3,2,1,0:T(8,128)(2,1)} %copy-done.1), custom_call_target="tpu_custom_call" | custom-call | tf_op jit(solution)/shard_map/gather/pallas_call | solution.py:202
  153.3 34.3 %correlate.1 = bf16[4,64,64,512]{3,2,1,0:T(8,128)(2,1)} custom-call(s32[4]{0:T(128)S(1)} %dynamic_slice.3.owner_ref, bf16[2,2,4,4,8,4,2,16,128]{8,7,6,5,4,3,2,1,0:T(8,128)(2,1)} %gather.1.source_ref.target_ref, bf16[2,2,4,4,8,4,2,16,128]{8,7,6,5,4,3,2,1,0:T(8,128)(2,1)} %gather.1.source_ref.target_ref), custom_call_target="tpu_custom_call" | custom-call | tf_op jit(solution)/shard_map/correlate/pallas_call | solution.py:264
Async XLA Ops:
  2.3 1.6 copy-start
  3.9 1.0 copy-start.2
  6.9 0.8 copy-start.1

commit v2 on v0

v2 whole, which is shorter than its diff:
```python
import functools
import math

import jax
import jax.numpy as jnp
import numpy as np
from jax import lax
from jax.experimental import pallas as pl
from jax.experimental.pallas import tpu as pltpu
from jax.sharding import PartitionSpec as P

SAMPLES = 2048
BINS = 256
LOW_BIN = 16
BLOCK = 64
TILES = 252
GROUPS = BINS // 8
CHUNKS = GROUPS // 4
COUNT = 2 * CHUNKS
ENTRIES = 16
NONE = 32
CAPS = (12, 14, 16)
AHEAD_ONE = 4
AHEAD_TWO = 3
AHEAD_FWD = 1
LAG = 4
STAGES = 8
MESH = pl.DeviceIdType.MESH
BF16 = jnp.bfloat16
F32 = jnp.float32


def twiddles():
    k = LOW_BIN + np.arange(BINS)[:, None]
    coarse = 2.0 * math.pi * ((k * 128 * np.arange(SAMPLES // 128)[None, :]) % SAMPLES) / SAMPLES
    fine = 2.0 * math.pi * ((k * np.arange(128)[None, :]) % SAMPLES) / SAMPLES
    both = np.concatenate([np.cos(coarse), np.sin(coarse)], axis=1)
    both = np.pad(both, ((0, 0), (0, 128 - both.shape[1])))
    return np.stack([both, np.cos(fine), np.sin(fine)]).astype(np.float32)


def fill_basis(table_ref, basis_ref):
    cos_fine, sin_fine = table_ref[1], table_ref[2]
    for step in range(SAMPLES // 128):
        cos_coarse = table_ref[0, :, step : step + 1]
        sin_coarse = table_ref[0, :, 16 + step : 17 + step]
        lanes = pl.ds(step * 128, 128)
        basis_ref[:BINS, lanes] = (cos_coarse * cos_fine - sin_coarse * sin_fine).astype(BF16)
        basis_ref[BINS:, lanes] = (-(sin_coarse * cos_fine + cos_coarse * sin_fine)).astype(BF16)


def transform(frame, basis_ref):
    spectrum = jnp.dot(basis_ref[...], frame, preferred_element_type=F32)
    power = jnp.sum(spectrum * spectrum, axis=0, keepdims=True) * (1.0 / (2 * BINS))
    return spectrum * lax.rsqrt(power + 1e-06)


def correlate(source, target):
    lane = lax.broadcasted_iota(jnp.int32, (BLOCK, 512), 1) % 8
    positive = lax.broadcasted_iota(jnp.int32, (256, 128), 1) < BLOCK
    sign = jnp.where(positive, 1.0, -1.0).astype(BF16)
    source = source.T
    left = jnp.concatenate([source[:BLOCK], source[BLOCK:]], axis=1)
    left = jnp.concatenate([jnp.where(lane == f, left, BF16(0)) for f in range(8)], axis=0)
    turned = jnp.concatenate([target[:, BLOCK:], target[:, :BLOCK]], axis=1)
    right = jnp.concatenate([target * sign, turned], axis=0)
    product = jnp.dot(left, right, preferred_element_type=F32) * (1.0 / 32)
    return jnp.swapaxes(product.reshape(8, BLOCK, 128), 0, 1)


def cross_kernel(cap, owner_ref, tiles_ref, table_ref, traces_ref, out_ref, *scratch):
    held = scratch[:COUNT]
    final = scratch[COUNT : 2 * COUNT]
    stage = scratch[2 * COUNT : 2 * COUNT + STAGES]
    cross, list_ref, place_ref, frames, basis, spec = scratch[2 * COUNT + STAGES : 2 * COUNT + STAGES + 6]
    (load_s, swap_s, swap_r, one_s, one_r, two_s, two_r, fwd_s, fwd_r,
     three_s, three_r, sib_s, sib_r, out_s) = scratch[2 * COUNT + STAGES + 6 :]
    src, rcv = lax.axis_index("src"), lax.axis_index("rcv")
    y, core, x, z = src // 2, src % 2, rcv // 4, rcv % 4

    def device(axis, step):
        if axis == "core":
            return (y * 2 + (1 - core), rcv)
        if axis == "x":
            return (src, (x + step) % 4 * 4 + z)
        if axis == "y":
            return ((y + step) % 4 * 2 + core, rcv)
        return (src, x * 4 + (z + step) % 4)

    partners = [device("core", 0)] + [device(a, s) for a in "xz" for s in (1, 2, 3)]
    partners += [device("y", 1), device("y", 3)]
    barrier = pltpu.get_barrier_semaphore()
    for partner in partners:
        pl.semaphore_signal(barrier, inc=1, device_id=partner, device_id_type=MESH)

    loads = [
        pltpu.make_async_copy(traces_ref.at[pl.ds(w * SAMPLES, SAMPLES)], frames.at[w], load_s.at[w])
        for w in range(2)
    ]
    for load in loads:
        load.start()
    fill_basis(table_ref, basis)
    whitened = []
    for w in range(2):
        loads[w].wait()
        whitened.append(transform(frames[w], basis))
    for block in range(4):
        lanes = slice(block * BLOCK, (block + 1) * BLOCK)
        rows = [
            jnp.concatenate([v[:BINS, lanes], v[BINS:, lanes]], axis=1).reshape(GROUPS, 8, 128)
            for v in whitened
        ]
        spec[block] = jnp.concatenate(rows, axis=1).astype(BF16)

    for n in range(COUNT):
        group = core * (GROUPS // 2) + n % 2 * CHUNKS + n // 2
        for block in range(4):
            held[n][y, (x, z)[n % 2], core * 4 + block] = spec[block, group]
    pl.semaphore_wait(barrier, len(partners))

    sent = []

    def send(source, target, send_sem, recv_sem, to, keep=True):
        copy = pltpu.make_async_remote_copy(
            src_ref=source, dst_ref=target, send_sem=send_sem, recv_sem=recv_sem,
            device_id=to, device_id_type=MESH,
        )
        copy.start()
        if keep:
            sent.append(copy)
        return copy

    swaps, ones, twos, forwards, threes, sibs, outs = {}, {}, {}, {}, {}, {}, {}

    def start_one(n):
        swaps[n].wait_recv()
        part = held[n].at[y, (x, z)[n % 2]]
        ones[n] = [
            send(part, part, one_s.at[n, s - 1], one_r.at[n, s - 1], device("xz"[n % 2], s))
            for s in (1, 3, 2)
        ]

    def start_two(n):
        for copy in ones[n]:
            copy.wait_recv()
        part = held[n].at[y]
        twos[n] = [
            send(part, part, two_s.at[n, i], two_r.at[n, i], device("y", s))
            for i, s in enumerate((1, 3))
        ]

    def start_forward(n):
        forwards[n] = []
        for i, s in enumerate((1, 3)):
            twos[n][i].wait_recv()
            part = held[n].at[(y - s) % 4, pl.ds(2 * i, 2)]
            forwards[n].append(send(part, part, fwd_s.at[n, i], fwd_r.at[n, i], device("y", s)))

    def start_three(n):
        q = n % 2
        for copy in forwards[n]:
            copy.wait_recv()
        last = (z, x)[q]
        parcel = stage[n % STAGES]
        if n >= STAGES:
            for copy in threes[n - STAGES]:
                copy.wait_send()

        def pick(row, r):
            block = list_ref[row, r]
            return held[n][block // 8, :, block % 8]

        @pl.loop(0, cap)
        def _(r):
            final[n][last, r] = pick(0, r)
            for s in (1, 2, 3):
                parcel[s - 1, r] = pick(s + 3 * q, r)

        threes[n] = [
            send(
                parcel.at[s - 1], final[n].at[last],
                three_s.at[n, s - 1], three_r.at[n, s - 1], device("zx"[q], s),
                keep=n >= COUNT - STAGES,
            )
            for s in (1, 3, 2)
        ]

    def finish(unit, mine):
        q, m = unit % 2, unit // 2
        pair = (4 * m + q, 4 * m + 2 + q)
        if not mine:
            for n in pair:
                for copy in threes[n]:
                    copy.wait_recv()
        if unit >= 2:
            if mine:
                outs[unit - 2].wait()
            else:
                sibs[unit - 2].wait_send()
        first = (core if mine else 1 - core) * 4
        there = out_ref.at[core * CHUNKS + q * (CHUNKS // 2) + m]
        buffer = cross.at[unit % 2, int(mine)]

        @pl.loop(0, 4, unroll=2)
        def _(j):
            parts = []
            for n in pair:
                source = final[n][:, place_ref[2 * (first + j)]].reshape(256, 128)
                target = final[n][:, place_ref[2 * (first + j) + 1]].reshape(256, 128)
                parts.append(correlate(source, target))
            buffer[j] = jnp.concatenate(parts, axis=1).astype(BF16)

        if mine:
            outs[unit] = pltpu.make_async_copy(buffer, there, out_s.at[unit])
            outs[unit].start()
        else:
            sibs[unit] = send(
                buffer, there, sib_s.at[unit], sib_r.at[unit], device("core", 0),
                keep=unit >= CHUNKS - 2,
            )

    for n in range(COUNT):
        group = (1 - core) * (GROUPS // 2) + n % 2 * CHUNKS + n // 2
        swaps[n] = send(
            spec.at[:, group], held[n].at[y, (x, z)[n % 2], pl.ds(core * 4, 4)],
            swap_s.at[n], swap_r.at[n], device("core", 0),
        )
    for n in range(AHEAD_ONE):
        start_one(n)
    for n in range(AHEAD_TWO):
        start_two(n)
        start_one(AHEAD_ONE + n)

    @pl.loop(0, 7)
    def _(turn_index):
        row = 6 - turn_index
        to_x = (x + jnp.where(row > 3, row - 3, 0)) % 4
        to_z = (z + jnp.where(row > 3, 0, row)) % 4
        blocks = []
        for slot in range(ENTRIES // 2):
            tile = owner_ref[((y * 2 + slot // 4) * 16 + to_x * 4 + to_z) * 4 + slot % 4]
            for role in range(2):
                block = tiles_ref[role, jnp.minimum(tile, TILES - 1)]
                blocks.append(jnp.where(tile < TILES, block, NONE))
        places = [jnp.int32(0)] * ENTRIES
        previous = jnp.int32(-1)
        for r in range(cap):
            current = jnp.int32(NONE)
            for block in blocks:
                current = jnp.minimum(current, jnp.where(block > previous, block, NONE))
            places = [p + jnp.where(current < b, 1, 0) for p, b in zip(places, blocks)]
            list_ref[row, r] = jnp.where(current < NONE, current, 0)
            previous = current
        for e in range(ENTRIES):
            place_ref[e] = jnp.minimum(places[e], cap - 1)

    for n in range(AHEAD_FWD):
        start_forward(n)
    work = [(u, mine) for u in range(CHUNKS) for mine in (False, True)]
    for n in range(COUNT):
        if n + AHEAD_ONE + AHEAD_TWO < COUNT:
            start_one(n + AHEAD_ONE + AHEAD_TWO)
        if n + AHEAD_TWO < COUNT:
            start_two(n + AHEAD_TWO)
        if n + AHEAD_FWD < COUNT:
            start_forward(n + AHEAD_FWD)
        start_three(n)
        u = work[0][0]
        if 4 * (u // 2) + 2 + u % 2 <= n - LAG:
            finish(*work.pop(0))
    while work:
        finish(*work.pop(0))
    for unit in range(CHUNKS):
        sibs[unit].wait_recv()
    for unit in (CHUNKS - 2, CHUNKS - 1):
        outs[unit].wait()
    for copy in sent:
        copy.wait_send()


def cross_spectra(cap, owner, tiles, traces):
    tail = (16, 128)
    dma = pltpu.SemaphoreType.DMA
    return pl.pallas_call(
        functools.partial(cross_kernel, cap),
        name=f"cross_{cap}",
        out_shape=jax.ShapeDtypeStruct((2 * CHUNKS, 4, BLOCK, 16, 128), BF16),
        in_specs=[
            pl.BlockSpec(memory_space=pltpu.SMEM),
            pl.BlockSpec(memory_space=pltpu.SMEM),
            pl.BlockSpec(memory_space=pltpu.VMEM),
            pl.BlockSpec(memory_space=pl.ANY),
        ],
        out_specs=pl.BlockSpec(memory_space=pl.ANY),
        scratch_shapes=[pltpu.VMEM((4, 4, 8) + tail, BF16)] * COUNT
        + [pltpu.VMEM((4, cap, 4) + tail, BF16)] * COUNT
        + [pltpu.VMEM((3, cap, 4) + tail, BF16)] * STAGES
        + [pltpu.VMEM((2, 2, 4, BLOCK, 16, 128), BF16)]
        + [pltpu.SMEM((7, cap), jnp.int32), pltpu.SMEM((ENTRIES,), jnp.int32)]
        + [pltpu.VMEM((2, SAMPLES, 4 * BLOCK), BF16)]
        + [pltpu.VMEM((2 * BINS, SAMPLES), BF16)]
        + [pltpu.VMEM((4, GROUPS) + tail, BF16)]
        + [dma((2,))]
        + [dma((COUNT,))] * 2
        + [dma((COUNT, 3))] * 2
        + [dma((COUNT, 2))] * 4
        + [dma((COUNT, 3))] * 2
        + [dma((CHUNKS,))] * 3,
        compiler_params=pltpu.CompilerParams(
            collective_id=cap, has_side_effects=True, vmem_limit_bytes=(28 + cap) * 2**20
        ),
    )(owner, tiles, twiddles(), traces)


def turn_kernel(rows, owner_ref, cross_ref, out_ref):
    first = (lax.axis_index("src") * 16 + lax.axis_index("rcv")) * 4
    filled = owner_ref[first + pl.program_id(0)] < TILES

    @pl.when(filled)
    def _():
        @pl.loop(0, rows, unroll=16)
        def _(i):
            turned = cross_ref[:, 0, i].reshape(BINS, 128).T
            out_ref[0, i, :, :BINS] = turned[:BLOCK]
            out_ref[0, i, :, BINS:] = turned[BLOCK:]

    @pl.when(jnp.logical_not(filled))
    def _():
        out_ref[...] = jnp.zeros_like(out_ref)


def turn(owner, cross):
    rows = BLOCK
    return pl.pallas_call(
        functools.partial(turn_kernel, rows),
        name="turn",
        out_shape=jax.ShapeDtypeStruct((4, BLOCK, BLOCK, 2 * BINS), BF16),
        grid_spec=pltpu.PrefetchScalarGridSpec(
            num_scalar_prefetch=1,
            grid=(4, BLOCK // rows),
            in_specs=[pl.BlockSpec((2 * CHUNKS, 1, rows, 16, 128), lambda s, i, own: (0, s, i, 0, 0))],
            out_specs=pl.BlockSpec((1, rows, BLOCK, 2 * BINS), lambda s, i, own: (s, i, 0, 0)),
        ),
        compiler_params=pltpu.CompilerParams(vmem_limit_bytes=60 * 2**20),
    )(owner, cross)


def most_blocks(owner, tiles):
    ones = jnp.left_shift(1, tiles[:, 0]) | jnp.left_shift(1, tiles[:, 1])
    picked = owner[:, None] == jnp.arange(TILES, dtype=jnp.int32)[None, :]
    named = jnp.sum(jnp.where(picked, ones[None, :], 0), axis=1).reshape(4, 2, 16, 4)
    named = lax.reduce(named, np.int32(0), lax.bitwise_or, (1, 3))
    return jnp.max(lax.population_count(named))


def per_device(traces, tile_list, tile_owner):
    def run(cap):
        return lambda traces, tiles, owner: turn(owner, cross_spectra(cap, owner, tiles, traces))

    most = most_blocks(tile_owner, tile_list)
    index = sum((most > cap).astype(jnp.int32) for cap in CAPS[:-1])
    return lax.switch(index, [run(cap) for cap in CAPS], traces, tile_list.T, tile_owner)


def solution(mesh):
    in_specs = (P("rcv", "src"), P(), P())
    out_specs = P(("src", "rcv"), None, None, None)
    return jax.shard_map(
        per_device, mesh=mesh, in_specs=in_specs, out_specs=out_specs, check_vma=False
    )
```

time: 715 us -> 134 us (0.19)
  waiting for transfers between devices: 335 us -> 0 us
  local copies, waits for them, and re-layouts: 222 us -> 1.11 us
  Pallas kernels: 0 us -> 128 us
  other arithmetic: 71.3 us -> 2.46 us
  matrix products: 60.7 us -> 0 us
  between operations: 13.5 us -> 1.31 us
    all_to_all x1 -> x0, waiting for transfers between devices: 297 us -> none  [per_device(): lax.all_to_all(outgoing, 'rcv', split_axis=1, concat_axis=0, tiled=True)]
    pallas_call x0 -> x2, Pallas kernels: none -> 128 us  [the longest x1 116 us: cross_spectra(): pl.pallas_call(functools.partial(cross_kernel, cap), name=f'cross_{cap}',...]
    dot_general x4 -> x0, local copies, waits for them, and re-layouts: 117 us -> none  [product(): jnp.einsum('wkif,wkjf->kijf', left, right, preferred_element_type=jnp.flo...]
    all_to_all x1 -> x0, local copies, waits for them, and re-layouts: 79.4 us -> none  [per_device(): lax.all_to_all(outgoing, 'rcv', split_axis=1, concat_axis=0, tiled=True)]
    dot_general x5 -> x0, matrix products: 60.7 us -> none  [the longest x4 59.4 us: product(): jnp.einsum('wkif,wkjf->kijf', left, right, preferred_element_type=jnp.flo...]
    all_gather x1 -> x0, waiting for transfers between devices: 38.3 us -> none  [per_device(): lax.all_gather(transform(traces, basis), 'src', axis=1, tiled=True)]
    div x1 -> x0, other arithmetic: 29.2 us -> none  [cross_pairs(): (product(source_re, target_re) + product(source_im, target_im)) / window_...]
    mul x1 -> x0, other arithmetic: 15.9 us -> none  [per_device(): return crossed * filled[:, None, None, None]]
  transfers between devices with their start and end apart: 2 -> 0, of which waited for: 2 -> 0; matrix products, arithmetic and copies ran while one was open for 0% -> 0% of each run, Pallas kernels for 0% -> 0%
where the time goes in v2:
time: 134 us; the launch traced here: 133 us
  Pallas kernels  128 us (96%)
  other arithmetic  2.46 us (2%)
    pallas_call x1, Pallas kernels, cross_spectra(): pl.pallas_call(functools.partial(cross_kernel, cap), name=f'cross_{cap}',...  116 us
    pallas_call x1, Pallas kernels, turn(): pl.pallas_call(functools.partial(turn_kernel, rows), name='turn', out_sha...  12.7 us

profile of v2, /device:TPU:1, one launch (start us, length us, event | category | flops | bytes accessed | tf_op | source)
XLA Modules:
  0.0 133.3 jit_solution(12603016788647866808)
XLA Ops:
  0.0 0.8 shift-left_or_fusion
  0.8 0.9 select_reduce_fusion
  1.7 0.1 reshape.20
  1.8 0.1 reduce_or.9
  1.9 0.6 popcnt_reduce_fusion
  3.9 129.4 %conditional.1 = (bf16[4,64,64,512]{3,2,1,0:T(8,128)(2,1)}) conditional(s32[]{:T(128)} %clamp.3, (s32[512]{0:T(512)}, s32[2,252]{1,0:T(2,128)}, bf16[4096,256]{1,0:T(8,128)(2,1)}) %tuple.30, (s32[512]{0:T(512)}, s32[2,252]{1,0:T(2,128)}, bf16[4096,256]{1,0:T(8,128)(2,1)}) %tuple.31, (s32[512]{0:T(512)}, ...), branch_computations={%region_3.4_spmd.clone, %region_4.5_spmd.clone, %region_5.6_spmd.c... | conditional | bytes 1581120 | solution.py:362
  3.9 0.0 copy-start.3
  3.9 0.0 copy-start.2
  3.9 1.0 copy-done.2
  4.9 115.7 %cross_12.1.cross_ref = bf16[16,4,64,16,128]{4,3,2,1,0:T(8,128)(2,1)} custom-call(s32[512]{0:T(512)} %get-tuple-element.58.owner_ref, s32[2,252]{1,0:T(2,128)} %get-tuple-element.59.tiles_ref, f32[3,256,128]{2,1,0:T(8,128)S(1)} %copy-done.2, bf16[4096,256]{1,0:T(8,128)(2,1)} %get-tuple-element.60.traces_ref), custom_call_target="tpu_custom_call" | custom-call | tf_op jit(solution)/shard_map/cond/branch_0_fun/cross_12/pallas_call | solution.py:284
  120.6 0.0 copy-done.3
  120.6 12.7 %turn.3 = bf16[4,64,64,512]{3,2,1,0:T(8,128)(2,1)} custom-call(s32[512]{0:T(512)S(1)} %copy-done.3, bf16[16,4,64,16,128]{4,3,2,1,0:T(8,128)(2,1)} %cross_12.1.cross_ref), custom_call_target="tpu_custom_call" | custom-call | tf_op jit(solution)/shard_map/cond/branch_0_fun/turn/pallas_call | solution.py:334
Async XLA Ops:
  3.9 116.7 %copy-start.3 = (s32[512]{0:T(512)S(1)}, s32[512]{0:T(512)}, u32[]{:S(2)}) copy-start(s32[512]{0:T(512)} %get-tuple-element.58.owner_ref) | copy-start | bytes 6148 | tf_op jit(solution)/shard_map/cond
  3.9 1.0 copy-start.2
